TPU v7x, 128 devices: a whole 4x4x4 slice. The times are simulated.
128 devices in a mesh: row: 16 (over x_hi, z, core), col: 8 (over y, x_lo).
Axes of the slice: x: 4 (x_hi: 2, x_lo: 2; x = x_hi * 2 + x_lo), y: 4, z: 4, core: 2. Of those that a mesh axis runs over, the one named last changes fastest.
Arguments:
- density: float32 [128, 16, 128, 128], P('row', 'col'), as said below
- hamiltonian: float32 [128, 16, 128, 128], P('row', 'col'), as said below
- neighbours: int32 [128, 16], P('row'), may hold values from 0 to 127, as said below
Outputs:
- new_density: float32 [128, 16, 128, 128], P('row', 'col')
- energy_density: float32 [128, 16, 128, 128], P('row', 'col')
Inputs may be any that keep to these rules, and one draw needn't show every extreme that they name: `neighbours`: every entry of row I is a block column within 7 of I, cyclically over 128; each row lists its own index I, entries that name no neighbour repeat I, and row I lists J exactly when row J lists I. `density`: the matrix that these blocks form is symmetric. `hamiltonian`: the matrix that these blocks form is symmetric.
All inputs are finite; a program needn't handle non-finite values.
Results may differ from a plain program's by a relative error of at most 0.0001.
Values sent between devices are 32-bit elements; how exact they have to be, the bound alone decides.
A program may use at most 192 MiB of HBM per device.

v0:
```python
import jax
import jax.numpy as jnp
from jax import lax
from jax.sharding import PartitionSpec as P

EXACT = lax.Precision.HIGHEST


def with_halo(block, sides, width):
    for axis, dim in sides:
        count = lax.axis_size(axis)
        forward = [(i, i + 1) for i in range(count - 1)]
        forward.append((count - 1, 0))
        backward = [(target, source) for source, target in forward]
        low = lax.ppermute(
            lax.slice_in_dim(block, block.shape[dim] - width, None, axis=dim), axis, forward
        )
        high = lax.ppermute(lax.slice_in_dim(block, 0, width, axis=dim), axis, backward)
        block = jnp.concatenate([low, block, high], axis=dim)
    return block


def band_panel(panel, global_rows, col_count, band_reach):
    per_class = panel.shape[1] // col_count
    slot_grid = jnp.arange(panel.shape[1], dtype=jnp.int32)[None, :]
    source = (
        slot_grid + global_rows[:, None] - band_reach
    ) % col_count * per_class + slot_grid // col_count
    return jnp.take_along_axis(panel, source[:, :, None, None], axis=1)


def right_blocks(halo_rows, global_rows, own_offset, col_index, col_count, band_reach):
    rows_dev = global_rows.shape[0]
    per_class = halo_rows.shape[1]
    class_slots = jnp.arange(per_class, dtype=jnp.int32)[None, :]
    pieces = []
    for offset in range(2 * band_reach):
        near_rows = halo_rows[offset : offset + rows_dev]
        left_offset = (col_index - (global_rows - band_reach + offset) + band_reach) % col_count
        band_slot = own_offset[:, None] + class_slots * col_count - offset + band_reach
        is_valid = ((band_slot >= 0) & (band_slot < 2 * band_reach)).astype(jnp.float32)
        slot_pick = jnp.clip((band_slot - left_offset[:, None]) // col_count, 0, per_class - 1)
        chosen = jnp.take_along_axis(near_rows, slot_pick[:, :, None, None], axis=1)
        pieces.append(chosen * is_valid[:, :, None, None])
    return jnp.stack(pieces)


def band_times(left_band, stacked, own_mask):
    product = jnp.einsum(
        "isab,siqbc->iqac", left_band, stacked, precision=EXACT, preferred_element_type=jnp.float32
    )
    return product * own_mask[:, :, None, None]


def body(density, hamiltonian, neighbours):
    rows_dev = density.shape[0]
    per_class = density.shape[1]
    col_count = lax.axis_size("col")
    slot_count = per_class * col_count
    band_reach = slot_count // 2
    total_rows = rows_dev * lax.axis_size("row")
    col_index = lax.axis_index("col")
    local_rows = jnp.arange(rows_dev, dtype=jnp.int32)
    global_rows = lax.axis_index("row") * rows_dev + local_rows
    own_offset = (col_index - global_rows + band_reach) % col_count
    class_slots = jnp.arange(per_class, dtype=jnp.int32)[None, :]
    own_cols = (
        global_rows[:, None] - band_reach + own_offset[:, None] + class_slots * col_count
    ) % total_rows
    own_mask = jnp.any(neighbours[:, None, :] == own_cols[:, :, None], axis=2).astype(jnp.float32)
    masked_density = density * own_mask[:, :, None, None]
    masked_hamiltonian = hamiltonian * own_mask[:, :, None, None]
    near_density = with_halo(masked_density, (("row", 0),), band_reach)
    density_right = right_blocks(
        near_density, global_rows, own_offset, col_index, col_count, band_reach
    )
    density_panel, hamiltonian_panel = (
        lax.all_gather(masked_density, "col", axis=1, tiled=True),
        lax.all_gather(masked_hamiltonian, "col", axis=1, tiled=True),
    )
    density_left = band_panel(density_panel, global_rows, col_count, band_reach)
    hamiltonian_left = band_panel(hamiltonian_panel, global_rows, col_count, band_reach)
    mixed = band_times(hamiltonian_left, density_right, own_mask)
    squared = band_times(density_left, density_right, own_mask)
    stacked_pair = jnp.stack([squared, mixed], axis=1)
    near_pair = with_halo(stacked_pair, (("row", 0),), band_reach)
    squared_right = right_blocks(
        near_pair[:, 0], global_rows, own_offset, col_index, col_count, band_reach
    )
    cubed = band_times(density_left, squared_right, own_mask)
    mixed_right = right_blocks(
        near_pair[:, 1], global_rows, own_offset, col_index, col_count, band_reach
    )
    energy_density = band_times(density_left, mixed_right, own_mask)
    new_density = 3.0 * squared - 2.0 * cubed
    return (new_density, energy_density)


def solution(mesh):
    placed = (P("row", "col", None, None), P("row", "col", None, None), P("row", None))
    return jax.shard_map(
        body,
        mesh=mesh,
        in_specs=placed,
        out_specs=(P("row", "col", None, None), P("row", "col", None, None)),
        check_vma=False,
    )
```

profile of v0, /device:TPU:97, one launch (start us, length us, event | category | flops | bytes accessed | tf_op | source)
XLA Modules:
  0.0 611.9 jit_solution(16973708681062876553)
XLA Ops:
  8.4 3.2 broadcast_multiply_fusion
  22.8 12.3 %collective-permute-done = f32[8,2,128,128]{3,2,1,0:T(8,128)S(1)} collective-permute-done((f32[8,2,128,128]{3,2,1,0:T(8,128)}, f32[8,2,128,128]{3,2,1,0:T(8,128)S(1)}, u32[]{:S(2)}, u32[]{:S(2)}) %collective-permute-start) | collective-permute-done | bytes 1048608 | tf_op jit(solution)/shard_map/ppermute | solution.py:15
  37.1 4.4 pad_maximum_fusion.3
  41.5 3.0 gather_fusion.1
  47.1 2.8 gather_fusion.2
  52.4 2.9 gather_fusion.3
  57.8 2.8 gather_fusion.4
  63.2 2.8 gather_fusion.5
  74.7 4.7 pad_maximum_fusion.2
  79.5 2.9 gather_fusion.9
  84.9 2.8 gather_fusion.10
  90.3 2.9 gather_fusion.11
  95.7 2.9 gather_fusion.12
  136.7 48.4 %all-gather.5.cloned.1.call-done = f32[8,16,128,128]{3,2,1,0:T(8,128)} async-done(((f32[8,2,128,128]{3,2,1,0:T(8,128)}), f32[8,16,128,128]{3,2,1,0:T(8,128)}) %all-gather.5.cloned.1.call-update) | async-done | bytes 8388624 | tf_op jit(solution)/shard_map/all_gather | solution.py:79
  185.2 7.8 %gather_fusion.17 = f32[128,128,128]{2,1,0:T(8,128)} fusion(f32[8,16,128,128]{3,2,1,0:T(8,128)} %all-gather.5.cloned.1.call-done, s32[128]{0:T(128)S(1)} %reshape.3530), kind=kCustom, calls=%fused_computation.49.clone | custom fusion | bytes 16778240 | tf_op jit(solution)/shard_map/jit(take_along_axis)/gather | solution.py:29
  192.9 20.3 %fusion.34 = f32[8,2,128,128]{3,2,1,0:T(8,128)S(1)} fusion(f32[16,8,2,128,128]{3,4,0,2,1:T(8,128)} %bitcast_dynamic-update-slice_fusion.47, f32[8,16,128,128]{3,2,1,0:T(8,128)} %bitcast.460, pred[8,16]{1,0:T(8,128)(4,1)S(1)} %and_bitcast_fusion, f32[8,2]{1,0:T(8,128)S(1)} %copy.269), kind=kOutput, calls=%fused_computation.100 | convolution fusion | flops 6444810240 | bytes 26214592 | tf_op jit(solution)/shard_map/isab,siqbc->iqac/dot_general | solution.py:49
  213.2 145.1 %all-gather.3.cloned.1.call-done = f32[8,16,128,128]{3,2,1,0:T(8,128)} async-done(((f32[8,2,128,128]{3,2,1,0:T(8,128)}), f32[8,16,128,128]{3,2,1,0:T(8,128)}) %all-gather.3.cloned.1.call-update) | async-done | bytes 8388624 | tf_op jit(solution)/shard_map/all_gather | solution.py:78
  358.3 7.8 %gather_fusion.16 = f32[128,128,128]{2,1,0:T(8,128)} fusion(f32[8,16,128,128]{3,2,1,0:T(8,128)} %all-gather.3.cloned.1.call-done, s32[128]{0:T(128)S(1)} %reshape.3530), kind=kCustom, calls=%fused_computation.1.clone | custom fusion | bytes 16778240 | tf_op jit(solution)/shard_map/jit(take_along_axis)/gather | solution.py:29
  366.1 20.0 %fusion.37 = f32[8,2,128,128]{3,2,1,0:T(8,128)S(1)} fusion(f32[16,8,2,128,128]{3,4,0,2,1:T(8,128)} %bitcast_dynamic-update-slice_fusion.47, f32[8,2]{1,0:T(8,128)S(1)} %copy.269, f32[8,16,128,128]{3,2,1,0:T(8,128)} %bitcast.455, pred[8,16]{0,1:T(8,128)(4,1)S(1)} %copy.332), kind=kOutput, calls=%fused_computation.101 | convolution fusion | flops 6444810240 | bytes 26214592 | tf_op jit(solution)/shard_map/isab,siqbc->iqac/dot_general | solution.py:49
  393.5 20.1 %collective-permute-done.2 = f32[8,2,2,128,128]{3,4,2,0,1:T(8,128)} collective-permute-done((f32[8,2,2,128,128]{3,4,2,0,1:T(8,128)}, f32[8,2,2,128,128]{3,4,2,0,1:T(8,128)}, u32[]{:S(2)}, u32[]{:S(2)}) %collective-permute-start.2) | collective-permute-done | bytes 2097184 | tf_op jit(solution)/shard_map/ppermute | solution.py:15
  413.5 6.1 collective-permute-done.3
  419.6 5.4 pad_maximum_fusion
  425.1 10.8 %slice_bitcast_fusion.7 = (f32[8,2,128,128]{2,3,1,0:T(8,128)S(1)}, f32[8,2,128,128]{2,3,1,0:T(8,128)}, f32[8,2,128,128]{2,3,1,0:T(8,128)}, f32[8,2,128,128]{2,3,...) fusion(f32[16,2,2,128,128]{3,4,2,0,1:T(8,128)} %get-tuple-eleme, ...), kind=kLoop, calls=%fused_computation.121 | loop fusion | bytes 29360128 | tf_op jit(solution)/shard_map/slice | solution.py:38
  435.9 2.8 gather_fusion.19
  438.7 2.8 gather_fusion.35
  441.5 3.1 slice_bitcast_fusion.14
  444.6 2.8 gather_fusion.18
  450.3 2.8 gather_fusion.20
  455.9 2.8 gather_fusion.21
  458.7 2.8 gather_fusion.37
  464.3 2.9 gather_fusion.38
  470.0 2.8 gather_fusion.39
  472.8 2.9 gather_fusion.24
  475.7 2.9 gather_fusion.40
  481.8 11.0 %slice_bitcast_fusion = (f32[8,2,128,128]{2,3,1,0:T(8,128)S(1)}, f32[8,2,128,128]{2,3,1,0:T(8,128)}, f32[8,2,128,128]{2,3,1,0:T(8,128)}, f32[8,2,128,128]{2,3,1,...) fusion(f32[16,2,2,128,128]{3,4,2,0,1:T(8,128)} %get-tuple-eleme, ...), kind=kLoop, calls=%fused_computation.114 | loop fusion | bytes 29360128 | tf_op jit(solution)/shard_map/slice | solution.py:38
  495.6 2.8 gather_fusion.43
  498.4 2.8 gather_fusion.28
  512.5 2.8 gather_fusion.46
  515.3 2.8 gather_fusion.31
  518.1 2.8 gather_fusion.47
  520.9 2.8 gather_fusion.32
  523.8 2.8 gather_fusion.48
  528.9 3.4 bitcast_dynamic-update-slice_fusion.30
  532.3 4.0 bitcast_dynamic-update-slice_fusion.29
  536.3 3.5 bitcast_dynamic-update-slice_fusion.28
  539.8 3.4 bitcast_dynamic-update-slice_fusion.27
  564.0 18.0 %fusion.29 = f32[8,2,128,128]{3,2,0,1:T(8,128)S(1)} fusion(f32[8,16,128,128]{3,2,1,0:T(8,128)S(1)} %bitcast.459, pred[8,16]{0,1:T(8,128)(4,1)S(1)} %copy.332, f32[16,8,2,128,128]{3,4,2,1,0:T(8,128)} %get-tuple-element.56), kind=kOutput, calls=%fused_computation.99 | convolution fusion | flops 6444548096 | bytes 26214528 | tf_op jit(solution)/shard_map/isab,siqbc->iqac/dot_general | solution.py:49
  583.5 19.6 %fusion.24 = f32[8,2,128,128]{3,2,0,1:T(8,128)S(1)} fusion(f32[8,16,128,128]{3,2,1,0:T(8,128)} %bitcast.456, pred[8,16]{0,1:T(8,128)(4,1)S(1)} %copy.332, f32[16,8,2,128,128]{3,4,2,1,0:T(8,128)} %get-tuple-element.57), kind=kOutput, calls=%fused_computation.98 | convolution fusion | flops 6444548096 | bytes 26214528 | tf_op jit(solution)/shard_map/isab,siqbc->iqac/dot_general | solution.py:49
  (228 shorter events, 140.6 us)
Async XLA Ops:
  7.2 178.0 %all-gather.5.cloned.1.call-start = ((), (), s32[]{:S(2)}) async-start(), calls=%async_computation.1 | async-start | bytes 9437184 | tf_op jit(solution)/shard_map/all_gather | solution.py:79
  11.6 346.7 %all-gather.3.cloned.1.call-start = ((), (), s32[]{:S(2)}) async-start(), calls=%async_computation | async-start | bytes 9437184 | tf_op jit(solution)/shard_map/all_gather | solution.py:78
  12.4 22.8 %collective-permute-start = (f32[8,2,128,128]{3,2,1,0:T(8,128)}, f32[8,2,128,128]{3,2,1,0:T(8,128)S(1)}, u32[]{:S(2)}, u32[]{:S(2)}) collective-permute-start(f32[8,2,128,128]{3,2,1,0:T(8,128)} %get-tuple-element.89), channel_id=1, source_target_pairs={{0,8},{8,16},{16,24},{24,32},{32,40},{40,48},{48,56},{56,64},{64,7... | collective-permute-start | bytes 3145736 | tf_op jit(solution)/shard_map/ppermute | solution.py:15
  14.4 60.4 %collective-permute-start.1 = (f32[8,2,128,128]{3,2,1,0:T(8,128)}, f32[8,2,128,128]{3,2,1,0:T(8,128)}, u32[]{:S(2)}, u32[]{:S(2)}) collective-permute-start(f32[8,2,128,128]{3,2,1,0:T(8,128)} %get-tuple-element.89), channel_id=1, source_target_pairs={{8,0},{16,8},{24,16},{32,24},{40,32},{48,40},{56,48},{64,56},{72,6... | collective-permute-start | bytes 3145736 | tf_op jit(solution)/shard_map/ppermute | solution.py:18
  41.5 33.3 %copy-start = (f32[8,2,128,128]{3,2,1,0:T(8,128)S(1)}, f32[8,2,128,128]{3,2,1,0:T(8,128)}, u32[]{:S(2)}) copy-start(f32[8,2,128,128]{3,2,1,0:T(8,128)} %get-tuple-element.89) | copy-start | bytes 3145732
  79.5 21.6 %copy-start.1 = (f32[8,2,128,128]{3,2,1,0:T(8,128)S(1)}, f32[8,2,128,128]{3,2,1,0:T(8,128)}, u32[]{:S(2)}) copy-start(f32[8,2,128,128]{3,2,1,0:T(8,128)} %get-tuple-element.47) | copy-start | bytes 3145732
  105.9 21.6 %copy-start.2 = (f32[16,128,128]{1,2,0:T(8,128)S(1)}, f32[16,128,128]{1,2,0:T(8,128)}, u32[]{:S(2)}) copy-start(f32[16,128,128]{1,2,0:T(8,128)} %copy.295) | copy-start | bytes 3145732
  107.8 18.5 %copy-start.3 = (f32[16,128,128]{1,2,0:T(8,128)S(1)}, f32[16,128,128]{1,2,0:T(8,128)}, u32[]{:S(2)}) copy-start(f32[16,128,128]{1,2,0:T(8,128)} %copy.292) | copy-start | bytes 3145732
  109.2 19.5 %copy-start.4 = (f32[16,128,128]{1,2,0:T(8,128)S(1)}, f32[16,128,128]{1,2,0:T(8,128)}, u32[]{:S(2)}) copy-start(f32[16,128,128]{1,2,0:T(8,128)} %copy.298) | copy-start | bytes 3145732
  109.2 20.6 %copy-start.5 = (f32[16,128,128]{1,2,0:T(8,128)S(1)}, f32[16,128,128]{1,2,0:T(8,128)}, u32[]{:S(2)}) copy-start(f32[16,128,128]{1,2,0:T(8,128)} %copy.301) | copy-start | bytes 3145732
  109.2 21.7 %copy-start.6 = (f32[16,128,128]{1,2,0:T(8,128)S(1)}, f32[16,128,128]{1,2,0:T(8,128)}, u32[]{:S(2)}) copy-start(f32[16,128,128]{1,2,0:T(8,128)} %copy.304) | copy-start | bytes 3145732
  109.2 22.9 %copy-start.7 = (f32[16,128,128]{1,2,0:T(8,128)S(1)}, f32[16,128,128]{1,2,0:T(8,128)}, u32[]{:S(2)}) copy-start(f32[16,128,128]{1,2,0:T(8,128)} %copy.307) | copy-start | bytes 3145732
  109.2 24.0 %copy-start.8 = (f32[16,128,128]{1,2,0:T(8,128)S(1)}, f32[16,128,128]{1,2,0:T(8,128)}, u32[]{:S(2)}) copy-start(f32[16,128,128]{1,2,0:T(8,128)} %copy.310) | copy-start | bytes 3145732
  109.2 25.2 %copy-start.9 = (f32[16,128,128]{1,2,0:T(8,128)S(1)}, f32[16,128,128]{1,2,0:T(8,128)}, u32[]{:S(2)}) copy-start(f32[16,128,128]{1,2,0:T(8,128)} %copy.313) | copy-start | bytes 3145732
  109.2 26.4 %copy-start.10 = (f32[16,128,128]{1,2,0:T(8,128)S(1)}, f32[16,128,128]{1,2,0:T(8,128)}, u32[]{:S(2)}) copy-start(f32[16,128,128]{1,2,0:T(8,128)} %copy.316) | copy-start | bytes 3145732
  387.5 26.0 %collective-permute-start.2 = (f32[8,2,2,128,128]{3,4,2,0,1:T(8,128)}, f32[8,2,2,128,128]{3,4,2,0,1:T(8,128)}, u32[]{:S(2)}, u32[]{:S(2)}) collective-permute-start(f32[8,2,2,128,128]{3,4,2,0,1:T(8,128)} %pad_maximum_fusion.1), channel_id=1, source_target_pairs={{0,8},{8,16},{16,24},{24,32},{32,40},{40,48},{48,56},{56,64},{64,7... | collective-permute-start | bytes 6291464 | tf_op jit(solution)/shard_map/ppermute | solution.py:15
  390.2 29.4 %collective-permute-start.3 = (f32[8,2,2,128,128]{3,4,2,0,1:T(8,128)}, f32[8,2,2,128,128]{3,4,2,0,1:T(8,128)}, u32[]{:S(2)}, u32[]{:S(2)}) collective-permute-start(f32[8,2,2,128,128]{3,4,2,0,1:T(8,128)} %pad_maximum_fusion.1), channel_id=1, source_target_pairs={{8,0},{16,8},{24,16},{32,24},{40,32},{48,40},{56,48},{64,56},{72,6... | collective-permute-start | bytes 6291464 | tf_op jit(solution)/shard_map/ppermute | solution.py:18
  528.8 14.5 %copy-start.32 = (f32[16,128,128]{1,2,0:T(8,128)S(1)}, f32[16,128,128]{1,2,0:T(8,128)}, u32[]{:S(2)}) copy-start(f32[16,128,128]{1,2,0:T(8,128)} %gather_fusion.22) | copy-start | bytes 3145732
  528.8 14.4 %copy-start.33 = (f32[16,128,128]{1,2,0:T(8,128)S(1)}, f32[16,128,128]{1,2,0:T(8,128)}, u32[]{:S(2)}) copy-start(f32[16,128,128]{1,2,0:T(8,128)} %gather_fusion.38) | copy-start | bytes 3145732
  528.8 16.2 %copy-start.30 = (f32[16,128,128]{1,2,0:T(8,128)S(1)}, f32[16,128,128]{1,2,0:T(8,128)}, u32[]{:S(2)}) copy-start(f32[16,128,128]{1,2,0:T(8,128)} %gather_fusion.23) | copy-start | bytes 3145732
  528.8 16.2 %copy-start.31 = (f32[16,128,128]{1,2,0:T(8,128)S(1)}, f32[16,128,128]{1,2,0:T(8,128)}, u32[]{:S(2)}) copy-start(f32[16,128,128]{1,2,0:T(8,128)} %gather_fusion.39) | copy-start | bytes 3145732
  528.8 18.0 %copy-start.28 = (f32[16,128,128]{1,2,0:T(8,128)S(1)}, f32[16,128,128]{1,2,0:T(8,128)}, u32[]{:S(2)}) copy-start(f32[16,128,128]{1,2,0:T(8,128)} %gather_fusion.24) | copy-start | bytes 3145732
  528.8 17.9 %copy-start.29 = (f32[16,128,128]{1,2,0:T(8,128)S(1)}, f32[16,128,128]{1,2,0:T(8,128)}, u32[]{:S(2)}) copy-start(f32[16,128,128]{1,2,0:T(8,128)} %gather_fusion.40) | copy-start | bytes 3145732
  528.9 19.8 %copy-start.24 = (f32[16,128,128]{1,2,0:T(8,128)S(1)}, f32[16,128,128]{1,2,0:T(8,128)}, u32[]{:S(2)}) copy-start(f32[16,128,128]{1,2,0:T(8,128)} %gather_fusion.25) | copy-start | bytes 3145732
  528.9 19.7 %copy-start.25 = (f32[16,128,128]{1,2,0:T(8,128)S(1)}, f32[16,128,128]{1,2,0:T(8,128)}, u32[]{:S(2)}) copy-start(f32[16,128,128]{1,2,0:T(8,128)} %gather_fusion.41) | copy-start | bytes 3145732
  528.9 21.5 %copy-start.11 = (f32[16,128,128]{1,2,0:T(8,128)S(1)}, f32[16,128,128]{1,2,0:T(8,128)}, u32[]{:S(2)}) copy-start(f32[16,128,128]{1,2,0:T(8,128)} %gather_fusion.26) | copy-start | bytes 3145732
  528.9 21.5 %copy-start.12 = (f32[16,128,128]{1,2,0:T(8,128)S(1)}, f32[16,128,128]{1,2,0:T(8,128)}, u32[]{:S(2)}) copy-start(f32[16,128,128]{1,2,0:T(8,128)} %gather_fusion.42) | copy-start | bytes 3145732
  532.3 19.8 %copy-start.26 = (f32[16,128,128]{1,2,0:T(8,128)S(1)}, f32[16,128,128]{1,2,0:T(8,128)}, u32[]{:S(2)}) copy-start(f32[16,128,128]{1,2,0:T(8,128)} %gather_fusion.27) | copy-start | bytes 3145732
  532.3 19.8 %copy-start.27 = (f32[16,128,128]{1,2,0:T(8,128)S(1)}, f32[16,128,128]{1,2,0:T(8,128)}, u32[]{:S(2)}) copy-start(f32[16,128,128]{1,2,0:T(8,128)} %gather_fusion.43) | copy-start | bytes 3145732
  536.3 17.5 %copy-start.22 = (f32[16,128,128]{1,2,0:T(8,128)S(1)}, f32[16,128,128]{1,2,0:T(8,128)}, u32[]{:S(2)}) copy-start(f32[16,128,128]{1,2,0:T(8,128)} %gather_fusion.28) | copy-start | bytes 3145732
  536.3 17.5 %copy-start.23 = (f32[16,128,128]{1,2,0:T(8,128)S(1)}, f32[16,128,128]{1,2,0:T(8,128)}, u32[]{:S(2)}) copy-start(f32[16,128,128]{1,2,0:T(8,128)} %gather_fusion.44) | copy-start | bytes 3145732
  539.8 15.7 %copy-start.20 = (f32[16,128,128]{1,2,0:T(8,128)S(1)}, f32[16,128,128]{1,2,0:T(8,128)}, u32[]{:S(2)}) copy-start(f32[16,128,128]{1,2,0:T(8,128)} %gather_fusion.29) | copy-start | bytes 3145732
  539.8 15.7 %copy-start.21 = (f32[16,128,128]{1,2,0:T(8,128)S(1)}, f32[16,128,128]{1,2,0:T(8,128)}, u32[]{:S(2)}) copy-start(f32[16,128,128]{1,2,0:T(8,128)} %gather_fusion.45) | copy-start | bytes 3145732
  543.3 14.1 %copy-start.18 = (f32[16,128,128]{1,2,0:T(8,128)S(1)}, f32[16,128,128]{1,2,0:T(8,128)}, u32[]{:S(2)}) copy-start(f32[16,128,128]{1,2,0:T(8,128)} %gather_fusion.30) | copy-start | bytes 3145732
  543.3 14.1 %copy-start.19 = (f32[16,128,128]{1,2,0:T(8,128)S(1)}, f32[16,128,128]{1,2,0:T(8,128)}, u32[]{:S(2)}) copy-start(f32[16,128,128]{1,2,0:T(8,128)} %gather_fusion.46) | copy-start | bytes 3145732
  545.0 14.0 %copy-start.16 = (f32[16,128,128]{1,2,0:T(8,128)S(1)}, f32[16,128,128]{1,2,0:T(8,128)}, u32[]{:S(2)}) copy-start(f32[16,128,128]{1,2,0:T(8,128)} %gather_fusion.31) | copy-start | bytes 3145732
  545.0 14.0 %copy-start.17 = (f32[16,128,128]{1,2,0:T(8,128)S(1)}, f32[16,128,128]{1,2,0:T(8,128)}, u32[]{:S(2)}) copy-start(f32[16,128,128]{1,2,0:T(8,128)} %gather_fusion.47) | copy-start | bytes 3145732
  546.8 13.9 %copy-start.14 = (f32[16,128,128]{1,2,0:T(8,128)S(1)}, f32[16,128,128]{1,2,0:T(8,128)}, u32[]{:S(2)}) copy-start(f32[16,128,128]{1,2,0:T(8,128)} %gather_fusion.32) | copy-start | bytes 3145732
  546.8 13.9 %copy-start.15 = (f32[16,128,128]{1,2,0:T(8,128)S(1)}, f32[16,128,128]{1,2,0:T(8,128)}, u32[]{:S(2)}) copy-start(f32[16,128,128]{1,2,0:T(8,128)} %gather_fusion.48) | copy-start | bytes 3145732
  548.6 13.8 %copy-start.13 = (f32[16,128,128]{1,2,0:T(8,128)S(1)}, f32[16,128,128]{1,2,0:T(8,128)}, u32[]{:S(2)}) copy-start(f32[16,128,128]{1,2,0:T(8,128)} %gather_fusion.33) | copy-start | bytes 3145732
  550.4 13.6 %slice-start = ((s8[8388608]{0:T(1024)(128)(4,1)}), s8[4194304]{0:T(1024)(128)(4,1)S(1)}, s32[]{:S(2)}) async-start(s8[8388608]{0:T(1024)(128)(4,1)} %bitcast.457), calls=%async_computation.2 | async-start | bytes 8388608
  557.3 6.7 %slice-start.1 = ((s8[8388608]{0:T(1024)(128)(4,1)}), s8[4194304]{0:T(1024)(128)(4,1)S(1)}, s32[]{:S(2)}) async-start(s8[8388608]{0:T(1024)(128)(4,1)} %bitcast.457), calls=%async_computation.3 | async-start | bytes 8388608
Sparse Core Ops, SparseCore 0:
  11.7 173.3 all-gather.4
  187.4 170.8 all-gather.2
where the time goes:
time: 623 us; the launch traced here: 612 us
  waiting for transfers between devices  233 us (37%)
  local copies, waits for them, and re-layouts  198 us (32%)
  other arithmetic  83.9 us (13%)
  matrix products  77.8 us (12%)
  between operations  14.9 us (2%)
    gather x96, local copies, waits for them, and re-layouts, right_blocks(): chosen = jnp.take_along_axis(near_rows, slot_pick[:, :, None, None], axis=1)  153 us
    all_gather x1, waiting for transfers between devices, body(): lax.all_gather(masked_density, 'col', axis=1, tiled=True)  145 us
    dot_general x4, matrix products, band_times(): jnp.einsum('isab,siqbc->iqac', left_band, stacked, precision=EXACT, prefe...  77.8 us
    unnamed x31, other arithmetic  59.7 us
    all_gather x1, waiting for transfers between devices, body(): lax.all_gather(masked_hamiltonian, 'col', axis=1, tiled=True)  48.4 us
    ppermute x2, waiting for transfers between devices, with_halo(): lax.ppermute(lax.slice_in_dim(block, block.shape[dim] - width, None, axis...  32.4 us
    slice x3, local copies, waits for them, and re-layouts, right_blocks(): near_rows = halo_rows[offset:offset + rows_dev]  24.9 us
    gather x3, local copies, waits for them, and re-layouts, band_panel(): return jnp.take_along_axis(panel, source[:, :, None, None], axis=1)  15.6 us
  transfers between devices with their start and end apart: 6, of which 5 were waited for; matrix products, arithmetic and copies ran while one was open for 23% of the time, Pallas kernels for 0%

commit v1 on v0

v1 whole, which is shorter than its diff:
```python
import functools
import jax
import jax.numpy as jnp
from jax import lax
from jax.experimental import pallas as pl
from jax.experimental.pallas import tpu as pltpu
from jax.sharding import PartitionSpec as P

MESH = pl.DeviceIdType.MESH
F32 = jnp.float32
BF16 = jnp.bfloat16
R8 = 8
N_ROW = 16
NB = 128
BW = 15
MID = 7
HALF = 4
GROUP = 3


def class_of(c, delta):
    if delta & 1:
        c = c + 1 - 2 * (c % 2)
    if delta & 2:
        c = c + 2 * (1 - 2 * ((c // 2) % 2))
    if delta & 4:
        c = c % 2 + 6 - 2 * (c // 2)
    return c


def slot_row(k, slot):
    e = slot - 4 * (slot // 5)
    wrap = (k + e) // 8
    i = (k + e) % 8
    is_off = slot // 5
    is_four = slot // 4 - is_off
    off = is_off * (1 - 2 * wrap) - is_four * wrap
    return i, off


def place(k, slot, c, base):
    i, off = slot_row(k, slot)
    a = i - c + MID + base
    b = k + 8 * off - c + MID + base
    ok = (a >= 0) & (a < BW) & (b >= 0) & (b < BW)
    return a, b, ok


def split(x):
    hi = x.astype(BF16)
    lo = (x - hi.astype(F32)).astype(BF16)
    return hi, lo


def kernel(
    d_ref, h_ref, nb_ref, new_ref, en_ref,
    gat, rel, hal, whi, wlo, xhi, xlo, x2hi, x2lo, sq, mx, rmx, oc, ro, msk,
    gss, grs, rss, rrs, hss, hrs, mss, mrs, oss, ors,
):
    bs = d_ref.shape[-1]
    r = lax.axis_index("row")
    c = lax.axis_index("col")
    up = (lax.rem(r + 1, N_ROW), c)
    down = (lax.rem(r + N_ROW - 1, N_ROW), c)

    def owner(a):
        t = c + 1 + a
        return (lax.rem(r + t // 8 - 1 + N_ROW, N_ROW), lax.rem(t, 8))

    barrier = pltpu.get_barrier_semaphore()
    for a in range(BW):
        if a != MID:
            pl.semaphore_signal(barrier, inc=1, device_id=owner(a), device_id_type=MESH)
    pl.semaphore_signal(barrier, inc=1, device_id=up, device_id_type=MESH)
    pl.semaphore_signal(barrier, inc=1, device_id=down, device_id_type=MESH)

    def rows(a):
        return pl.ds(pl.multiple_of(a * bs, bs), bs)

    def own_slot(i):
        return jnp.where(i <= c, 1, 0)

    col_mine = (8 * r + c - MID + NB + lax.broadcasted_iota(jnp.int32, (16, 16), 0)) % NB
    hit = jnp.where(nb_ref[pl.ds(c, 1), :] == col_mine, 1.0, 0.0).astype(F32)
    msk[0:16, :] = jnp.broadcast_to(jnp.max(hit, axis=1, keepdims=True), (16, bs))
    row_i = lax.broadcasted_iota(jnp.int32, (8, 16), 0)
    col_other = (8 * r + c + NB + jnp.where(row_i > c, 8, -8)) % NB
    hit = jnp.where(nb_ref[...] == col_other, 1.0, 0.0).astype(F32)
    msk[16:24, :] = jnp.broadcast_to(jnp.max(hit, axis=1, keepdims=True), (8, bs))

    def contribute(slot, _):
        i, off = slot_row(c, slot)
        other = off * off
        mine = own_slot(i)
        t = mine + other - 2 * mine * other
        m = msk[pl.ds((1 - other) * (i - c + MID) + other * (16 + i), 1), :]
        gat[c, slot] = d_ref[i, t] * m
        return 0

    lax.fori_loop(0, 8, contribute, 0)
    pl.semaphore_wait(barrier, 16)

    sends = []

    def part(k, p):
        return gat.at[k, pl.ds(HALF * p, HALF)]

    counts = [0, 0]

    def start_forward(p, delta, dim):
        k = class_of(c, delta)
        cp = pltpu.make_async_remote_copy(
            src_ref=part(k, p), dst_ref=part(k, p),
            send_sem=gss.at[p, counts[p]], recv_sem=grs.at[p, delta ^ dim],
            device_id=(r, class_of(c, dim)), device_id_type=MESH,
        )
        counts[p] += 1
        cp.start()
        sends.append(cp)

    order = {0: (1, 2, 4), 1: (1, 4, 2)}

    def dims_after(p, delta):
        o = order[p]
        last = max([o.index(d) for d in o if delta & d], default=-1)
        return o[last + 1:]

    for n in range(3):
        for p in (0, 1):
            start_forward(p, 0, order[p][n])

    def send_h(i, _):
        @pl.when(i != c)
        def _():
            t = 1 - own_slot(i)
            pltpu.make_async_remote_copy(
                src_ref=h_ref.at[i, t], dst_ref=hal.at[i],
                send_sem=hss.at[i], recv_sem=hrs.at[i],
                device_id=(lax.rem(r + jnp.where(i > c, 1, N_ROW - 1), N_ROW), c), device_id_type=MESH,
            ).start()
        return 0

    lax.fori_loop(0, 8, send_h, 0)

    def relay_copy(k, slot, is_up):
        return pltpu.make_async_remote_copy(
            src_ref=gat.at[k, slot], dst_ref=rel.at[k, slot],
            send_sem=rss.at[k, slot], recv_sem=rrs.at[k, slot],
            device_id=(lax.rem(r + jnp.where(is_up, 1, N_ROW - 1), N_ROW), c), device_id_type=MESH,
        )

    def put(x, a, b):
        hi, lo = split(x)
        whi[rows(a), rows(b)] = hi
        wlo[rows(a), rows(b)] = lo
        hi, lo = split(x.T)
        whi[rows(b), rows(a)] = hi
        wlo[rows(b), rows(a)] = lo

    def relay_part(k, p):
        def step(j, _):
            slot = HALF * p + j
            _, _, is_up = place(k, slot, c, -8)
            _, _, is_down = place(k, slot, c, 8)

            @pl.when(is_up | is_down)
            def _():
                relay_copy(k, slot, is_up).start()
            return 0

        lax.fori_loop(0, HALF, step, 0)

    def put_part(k, p):
        def step(j, _):
            slot = HALF * p + j
            a, b, ok = place(k, slot, c, 0)

            @pl.when(ok)
            def _():
                put(gat[k, slot], a, b)
            return 0

        lax.fori_loop(0, HALF, step, 0)

    for p in (0, 1):
        relay_part(c, p)

    zero = jnp.zeros((bs, bs), BF16)
    for g in range(BW // GROUP):
        lo_b, hi_b = max(0, GROUP * g - MID), min(BW - 1, GROUP * g + GROUP - 1 + MID)
        for a in range(GROUP * g, GROUP * g + GROUP):
            for b in range(lo_b, hi_b + 1):
                if abs(a - b) > MID:
                    whi[a * bs:(a + 1) * bs, b * bs:(b + 1) * bs] = zero
                    wlo[a * bs:(a + 1) * bs, b * bs:(b + 1) * bs] = zero
    for p in (0, 1):
        put_part(c, p)

    def arrive(p, delta):
        k = class_of(c, delta)
        pltpu.make_async_remote_copy(
            src_ref=part(k, p), dst_ref=part(k, p),
            send_sem=gss.at[p, 0], recv_sem=grs.at[p, delta],
            device_id=(r, class_of(c, 1)), device_id_type=MESH,
        ).wait_recv()
        for dim in dims_after(p, delta):
            start_forward(p, delta, dim)
        relay_part(k, p)

    events = [(0, 1), (1, 1), (0, 2), (1, 4), (0, 3), (1, 5), (0, 4), (1, 2), (0, 5), (1, 3), (0, 6), (1, 6), (0, 7), (1, 7)]
    pending = None
    for p, delta in events:
        arrive(p, delta)
        if pending is not None:
            put_part(*pending)
        pending = (class_of(c, delta), p)
    put_part(*pending)

    def put_h(x, a):
        hi, lo = split(x * msk[pl.ds(a, 1), :])
        xhi[rows(a), bs:2 * bs] = hi
        xlo[rows(a), bs:2 * bs] = lo

    def h_copy(i):
        return pltpu.make_async_remote_copy(
            src_ref=h_ref.at[i, 0], dst_ref=hal.at[i],
            send_sem=hss.at[i], recv_sem=hrs.at[i],
            device_id=up, device_id_type=MESH,
        )

    def take_h(i, _):
        put_h(h_ref[i, own_slot(i)], i - c + MID)

        @pl.when(i != c)
        def _():
            h_copy(i).wait_recv()
            put_h(hal[i], i - c + jnp.where(i > c, -1, 15))
        return 0

    lax.fori_loop(0, 8, take_h, 0)

    def take_relay(n, _):
        k = n // 8
        slot = n % 8
        a0, b0, below = place(k, slot, c, -8)
        a1, b1, above = place(k, slot, c, 8)

        @pl.when(below | above)
        def _():
            relay_copy(k, slot, below).wait_recv()
            put(rel[k, slot], jnp.where(below, a0, a1), jnp.where(below, b0, b1))
        return 0

    lax.fori_loop(0, 64, take_relay, 0)

    xhi[:, 0:bs] = whi[:, MID * bs:(MID + 1) * bs]
    xlo[:, 0:bs] = wlo[:, MID * bs:(MID + 1) * bs]

    def product(g, vhi, vlo):
        lo_b, hi_b = max(0, GROUP * g - MID), min(BW - 1, GROUP * g + GROUP - 1 + MID)
        rs = slice(GROUP * g * bs, GROUP * (g + 1) * bs)
        ks = slice(lo_b * bs, (hi_b + 1) * bs)
        dot = functools.partial(jnp.dot, preferred_element_type=F32)
        return dot(whi[rs, ks], vhi[ks, :]) + dot(whi[rs, ks], vlo[ks, :]) + dot(wlo[rs, ks], vhi[ks, :])

    def mx_copy(a, back):
        return pltpu.make_async_remote_copy(
            src_ref=mx.at[a], dst_ref=rmx.at[back],
            send_sem=mss.at[a], recv_sem=mrs.at[back],
            device_id=owner(a), device_id_type=MESH,
        )

    for g in range(BW // GROUP):
        y = product(g, xhi, xlo)
        for n in range(GROUP):
            a = GROUP * g + n
            m = msk[a:a + 1, :]
            s = y[n * bs:(n + 1) * bs, 0:bs] * m
            sq[a] = s
            hi, lo = split(s)
            x2hi[a * bs:(a + 1) * bs, 0:bs] = hi
            x2lo[a * bs:(a + 1) * bs, 0:bs] = lo
            mx[a] = y[n * bs:(n + 1) * bs, bs:2 * bs] * m
            if a != MID:
                mx_copy(a, BW - 1 - a).start()

    def put_mx(x, a):
        hi, lo = split(x.T)
        x2hi[rows(a), bs:2 * bs] = hi
        x2lo[rows(a), bs:2 * bs] = lo

    put_mx(mx[MID], MID)
    for a in range(BW):
        if a != MID:
            mx_copy(BW - 1 - a, a).wait_recv()
            put_mx(rmx[a], a)

    def out_copy(a):
        t = c + 1 + a
        return pltpu.make_async_remote_copy(
            src_ref=oc.at[a], dst_ref=ro.at[lax.rem(t, 8)],
            send_sem=oss.at[a], recv_sem=ors.at[lax.rem(t, 8)],
            device_id=(lax.rem(r + t // 8 - 1 + N_ROW, N_ROW), c), device_id_type=MESH,
        )

    for g in range(BW // GROUP):
        y = product(g, x2hi, x2lo)
        for n in range(GROUP):
            a = GROUP * g + n
            m = msk[a:a + 1, :]
            oc[a, 0] = 3.0 * sq[a] - 2.0 * (y[n * bs:(n + 1) * bs, 0:bs] * m)
            oc[a, 1] = y[n * bs:(n + 1) * bs, bs:2 * bs] * m
            if a != MID:
                @pl.when((c + 1 + a < 8) | (c + 1 + a >= 16))
                def _():
                    out_copy(a).start()

    def finish(i, _):
        t = own_slot(i)
        new_ref[i, t] = oc[i - c + MID, 0]
        en_ref[i, t] = oc[i - c + MID, 1]

        @pl.when(i == c)
        def _():
            new_ref[i, 0] = jnp.zeros((bs, bs), F32)
            en_ref[i, 0] = jnp.zeros((bs, bs), F32)

        @pl.when(i != c)
        def _():
            pltpu.make_async_remote_copy(
                src_ref=oc.at[0], dst_ref=ro.at[i],
                send_sem=oss.at[0], recv_sem=ors.at[i],
                device_id=up, device_id_type=MESH,
            ).wait_recv()
            new_ref[i, 1 - t] = ro[i, 0]
            en_ref[i, 1 - t] = ro[i, 1]
        return 0

    lax.fori_loop(0, 8, finish, 0)

    for cp in sends:
        cp.wait_send()

    def sent_h(i, _):
        @pl.when(i != c)
        def _():
            h_copy(i).wait_send()
        return 0

    lax.fori_loop(0, 8, sent_h, 0)

    def sent_relay(n, _):
        k = n // 8
        slot = n % 8
        _, _, is_up = place(k, slot, c, -8)
        _, _, is_down = place(k, slot, c, 8)

        @pl.when(is_up | is_down)
        def _():
            relay_copy(k, slot, is_up).wait_send()
        return 0

    lax.fori_loop(0, 64, sent_relay, 0)
    for a in range(BW):
        if a != MID:
            mx_copy(a, BW - 1 - a).wait_send()

            @pl.when((c + 1 + a < 8) | (c + 1 + a >= 16))
            def _():
                out_copy(a).wait_send()


def body(density, hamiltonian, neighbours):
    bs = density.shape[-1]
    block = (bs, bs)
    wide = (BW * bs, BW * bs)
    tall = (BW * bs, 2 * bs)
    vm = pl.BlockSpec(memory_space=pltpu.VMEM)
    dma = pltpu.SemaphoreType.DMA
    out = jax.ShapeDtypeStruct(density.shape, F32)
    return pl.pallas_call(
        kernel,
        out_shape=(out, out),
        in_specs=[vm] * 3,
        out_specs=(vm, vm),
        scratch_shapes=[
            pltpu.VMEM((8, 8) + block, F32),
            pltpu.VMEM((8, 8) + block, F32),
            pltpu.VMEM((8,) + block, F32),
            pltpu.VMEM(wide, BF16),
            pltpu.VMEM(wide, BF16),
            pltpu.VMEM(tall, BF16),
            pltpu.VMEM(tall, BF16),
            pltpu.VMEM(tall, BF16),
            pltpu.VMEM(tall, BF16),
            pltpu.VMEM((BW,) + block, F32),
            pltpu.VMEM((BW,) + block, F32),
            pltpu.VMEM((BW,) + block, F32),
            pltpu.VMEM((BW, 2) + block, F32),
            pltpu.VMEM((8, 2) + block, F32),
            pltpu.VMEM((24, bs), F32),
            dma((2, 7)), dma((2, 8)),
            dma((8, 8)), dma((8, 8)),
            dma((8,)), dma((8,)),
            dma((BW,)), dma((BW,)),
            dma((BW,)), dma((8,)),
        ],
        compiler_params=pltpu.CompilerParams(
            collective_id=0, has_side_effects=True, vmem_limit_bytes=56 * 2**20
        ),
        cost_estimate=pl.CostEstimate(flops=9 * 10**9, bytes_accessed=4 * 2**20, transcendentals=0),
        name="purify",
    )(density, hamiltonian, neighbours)


def solution(mesh):
    placed = (P("row", "col", None, None), P("row", "col", None, None), P("row", None))
    return jax.shard_map(
        body,
        mesh=mesh,
        in_specs=placed,
        out_specs=(P("row", "col", None, None), P("row", "col", None, None)),
        check_vma=False,
    )
```

time: 623 us -> 104 us (0.17)
  the two profiles are of different devices: /device:TPU:97 before, /device:TPU:26 now
where the time goes in v1:
time: 104 us
  Pallas kernels  100 us (96%)
  local copies, waits for them, and re-layouts  3.36 us (3%)
    pallas_call x1, Pallas kernels, body(): pl.pallas_call(kernel, out_shape=(out, out), in_specs=[vm] * 3, out_specs...  100 us
    unnamed x4, local copies, waits for them, and re-layouts  3.36 us

profile of v1, /device:TPU:26, one launch (start us, length us, event | category | flops | bytes accessed | tf_op | source)
XLA Modules:
  0.0 104.3 jit_solution(16997406593244817428)
XLA Ops:
  0.6 100.3 %purify.1 = (f32[8,2,128,128]{3,2,1,0:T(8,128)}, f32[8,2,128,128]{3,2,1,0:T(8,128)}) custom-call(f32[8,2,128,128]{3,2,1,0:T(8,128)} %d_ref.1, f32[8,2,128,128]{3,2,1,0:T(8,128)} %h_ref.1, s32[8,16]{1,0:T(8,128)} %nb_ref.1), custom_call_target="tpu_custom_call" | custom-call | flops 8999999488 | bytes 4194304 | tf_op jit(solution)/shard_map/purify/pallas_call | solution.py:381
  101.0 0.0 copy-start
  101.0 2.4 %copy.7 = f32[8,2,128,128]{3,2,1,0:T(8,128)} copy(f32[8,2,128,128]{3,2,1,0:T(8,128)} %get-tuple-element.4) | data formatting | bytes 2097152
  103.4 0.0 copy-done
  103.4 1.0 copy.8
Async XLA Ops:
  101.0 2.4 %copy-start = (f32[8,2,128,128]{3,2,1,0:T(8,128)S(1)}, f32[8,2,128,128]{3,2,1,0:T(8,128)}, u32[]{:S(2)}) copy-start(f32[8,2,128,128]{3,2,1,0:T(8,128)} %get-tuple-element.5) | copy-start | bytes 3145732

commit v2 on v1

v2 whole, which is shorter than its diff:
```python
import functools
import jax
import jax.numpy as jnp
from jax import lax
from jax.experimental import pallas as pl
from jax.experimental.pallas import tpu as pltpu
from jax.sharding import PartitionSpec as P

MESH = pl.DeviceIdType.MESH
F32 = jnp.float32
BF16 = jnp.bfloat16
R8 = 8
N_ROW = 16
NB = 128
BW = 15
MID = 7
GATHER = tuple(((1, 2, 4), (4, 1, 2), (2, 4, 1))[n % 3] for n in range(8))
SPREAD = ((4, 2, 1), (2, 4, 1), (2, 4, 1), (4, 2, 1), (1, 2, 4), (4, 2, 1), (1, 2, 4), (1, 2, 4))
GROUPS = (0, 4, 1, 3, 2)
GROUP = 3


def class_of(c, delta):
    if delta & 1:
        c = c + 1 - 2 * (c % 2)
    if delta & 2:
        c = c + 2 * (1 - 2 * ((c // 2) % 2))
    if delta & 4:
        c = c % 2 + 6 - 2 * (c // 2)
    return c


def slot_row(k, slot):
    if isinstance(slot, int):
        t = k + (slot - 4 if slot > 4 else slot)
    else:
        t = k + jnp.where(slot > 4, slot - 4, slot)
    wrapped = t >= 8
    i = jnp.where(wrapped, t - 8, t)
    if isinstance(slot, int):
        if slot < 4:
            return i, 0
        return i, jnp.where(wrapped, -1, 0 if slot == 4 else 1)
    return i, jnp.where(wrapped & (slot >= 4), -1, jnp.where(slot > 4, 1, 0))


def limits(k, slot):
    i, off = slot_row(k, slot)
    under, over = jnp.minimum(k, i), jnp.maximum(k, i)
    if not isinstance(off, int):
        under = jnp.where(off == 0, under, jnp.where(off > 0, i, 0))
        over = jnp.where(off == 0, over, jnp.where(off < 0, i, 7))
    return i, off, under, over


def dims_after(o, delta):
    last = max([n for n in range(3) if delta & o[n]], default=-1)
    return o[last + 1:]


def subtree(o, delta):
    found = [delta]
    for d in dims_after(o, delta):
        found += [x | d for x in found]
    return found


def split(x):
    hi = x.astype(BF16)
    lo = (x - hi.astype(F32)).astype(BF16)
    return hi, lo


def kernel(
    d_ref, h_ref, nb_ref, new_ref, en_ref,
    gat, rel, ext, hal, whi, wlo, xhi, xlo, x2s, x2m, sq, mx, rmx, oc, ro, msk,
    gss, grs, rss, rrs, ess, ers, zss, hss, hrs, mss, mrs, oss, ors,
):
    bs = d_ref.shape[-1]
    r = lax.axis_index("row")
    c = lax.axis_index("col")
    above = jnp.where(r == N_ROW - 1, 0, r + 1)
    below = jnp.where(r == 0, N_ROW - 1, r - 1)
    up = (above, c)
    down = (below, c)
    cls = [class_of(c, delta) for delta in range(8)]

    def owner(a):
        t = c + 1 + a
        row = jnp.where(t < 8, below, jnp.where(t < 16, r, above))
        return (row, jnp.where(t < 8, t, jnp.where(t < 16, t - 8, t - 16)))

    barrier = pltpu.get_barrier_semaphore()
    for a in range(BW):
        if a != MID:
            pl.semaphore_signal(barrier, inc=1, device_id=owner(a), device_id_type=MESH)
    pl.semaphore_signal(barrier, inc=1, device_id=up, device_id_type=MESH)
    pl.semaphore_signal(barrier, inc=1, device_id=down, device_id_type=MESH)

    def rows(a):
        return pl.ds(pl.multiple_of(a * bs, bs), bs)

    def own_slot(i):
        return jnp.where(i <= c, 1, 0)

    col_mine = (8 * r + c - MID + NB + lax.broadcasted_iota(jnp.int32, (16, 16), 0)) % NB
    hit = jnp.where(nb_ref[pl.ds(c, 1), :] == col_mine, 1.0, 0.0).astype(F32)
    msk[0:16, :] = jnp.broadcast_to(jnp.max(hit, axis=1, keepdims=True), (16, bs))
    row_i = lax.broadcasted_iota(jnp.int32, (8, 16), 0)
    col_other = (8 * r + c + NB + jnp.where(row_i > c, 8, -8)) % NB
    hit = jnp.where(nb_ref[...] == col_other, 1.0, 0.0).astype(F32)
    msk[16:24, :] = jnp.broadcast_to(jnp.max(hit, axis=1, keepdims=True), (8, bs))

    def contribute(slot, _):
        i, off = slot_row(c, slot)
        mine = own_slot(i)
        t = jnp.where(off == 0, mine, 1 - mine)
        m = msk[pl.ds(jnp.where(off == 0, i - c + MID, 16 + i), 1), :]
        gat[c, slot] = d_ref[i, t] * m
        return 0

    lax.fori_loop(0, 8, contribute, 0)
    pl.semaphore_wait(barrier, 16)

    sends = []
    counts = [0] * 8
    in_x_half = (r // 2) % 4
    low = 1 - lax.rem(r, 2)
    crossing = jnp.where(in_x_half == jnp.where(low == 1, 0, 3), 1, 0)

    def start_forward(slot, delta, dim):
        k = cls[delta]
        cp = pltpu.make_async_remote_copy(
            src_ref=gat.at[k, slot], dst_ref=gat.at[k, slot],
            send_sem=gss.at[slot, counts[slot]], recv_sem=grs.at[slot, delta ^ dim],
            device_id=(r, cls[dim]), device_id_type=MESH,
        )
        counts[slot] += 1
        cp.start()
        sends.append(cp)

    for slot in range(8):
        start_forward(slot, 0, GATHER[slot][0])

    beyond_r = jnp.where(low == 1, below, above)

    def reach(k, slot, is_low):
        i, off, under, over = limits(k, slot)
        found = jnp.where(is_low == 1, under, 7 - over)
        return jnp.where((crossing == 1) | (off != 0), found, 0)

    def cross_copy(slot):
        return pltpu.make_async_remote_copy(
            src_ref=gat.at[c, slot], dst_ref=ext.at[c, slot],
            send_sem=zss.at[slot], recv_sem=ers.at[c, slot],
            device_id=(beyond_r, c), device_id_type=MESH,
        )

    for slot in range(8):
        @pl.when(reach(c, slot, 1 - low) > 0)
        def _():
            cross_copy(slot).start()

    for slot in range(8):
        start_forward(slot, 0, GATHER[slot][1])

    dist = [jnp.where(low == 1, k, 7 - k) for k in cls]
    reached = {}

    def neediest(o, delta, dim):
        nodes = frozenset(delta ^ x for x in subtree(o, delta | dim))
        if nodes not in reached:
            reached[nodes] = functools.reduce(jnp.minimum, [dist[x] for x in sorted(nodes)])
        return reached[nodes]

    mine = dist[0]
    base = jnp.where(low == 1, -8, 8)
    def spread_copy(k, slot, dim, n):
        return pltpu.make_async_remote_copy(
            src_ref=ext.at[k, slot], dst_ref=ext.at[k, slot],
            send_sem=ess.at[k, slot, n], recv_sem=ers.at[k, slot],
            device_id=(r, cls[dim]), device_id_type=MESH,
        )

    onward = {}

    def spread(pick):
        for slot in range(8):
            o = SPREAD[slot]
            delta = pick(o)
            k = cls[delta]
            here = neediest(o, delta, 0)
            if (o, delta) not in onward:
                onward[o, delta] = [(dim, neediest(o, delta, dim)) for dim in dims_after(o, delta)]
            need = reach(k, slot, low)

            @pl.when(here < need)
            def _():
                spread_copy(k, slot, 1, 0).wait_recv()
                for n, (dim, v) in enumerate(onward[o, delta]):
                    @pl.when(v < need)
                    def _():
                        spread_copy(k, slot, dim, n).start()

    def spread_sent(slot, delta):
        o = SPREAD[slot]
        k = cls[delta]
        need = reach(k, slot, low)
        for n, (dim, v) in enumerate(onward[o, delta]):
            @pl.when((neediest(o, delta, 0) < need) & (v < need))
            def _():
                spread_copy(k, slot, dim, n).wait_send()

    def class_at(orders, pick, slot):
        deltas = [pick(o) for o in orders]
        k = cls[deltas[0]]
        for delta in sorted(set(deltas) - {deltas[0]}):
            hit = functools.reduce(jnp.logical_or, [slot == n for n in range(8) if deltas[n] == delta])
            k = jnp.where(hit, cls[delta], k)
        return k

    def put_spread(pick):
        def step(slot, _):
            k = class_at(SPREAD, pick, slot)

            @pl.when(mine < reach(k, slot, low))
            def _():
                i, off = slot_row(k, slot)
                put(ext[k, slot], i - c + MID + base, k + 8 * off - c + MID + base)
            return 0

        lax.fori_loop(0, 8, step, 0)

    def send_h(i, _):
        @pl.when(i != c)
        def _():
            t = 1 - own_slot(i)
            pltpu.make_async_remote_copy(
                src_ref=h_ref.at[i, t], dst_ref=hal.at[i],
                send_sem=hss.at[i], recv_sem=hrs.at[i],
                device_id=(jnp.where(i > c, above, below), c), device_id_type=MESH,
            ).start()
        return 0

    lax.fori_loop(0, 8, send_h, 0)

    def relayed(k, slot, inner_up):
        i, off, under, over = limits(k, slot)
        plain = (off == 0) & (crossing == 0)
        return i, off, (c < under) & (plain | (inner_up == 1)), (c > over) & (plain | (inner_up == 0))

    def relay_copy(k, slot, is_up):
        return pltpu.make_async_remote_copy(
            src_ref=gat.at[k, slot], dst_ref=rel.at[k, slot],
            send_sem=rss.at[k, slot], recv_sem=rrs.at[k, slot],
            device_id=(jnp.where(is_up, above, below), c), device_id_type=MESH,
        )

    def put(x, a, b):
        hi, lo = split(x)
        whi[rows(a), rows(b)] = hi
        wlo[rows(a), rows(b)] = lo
        hi, lo = split(x.T)
        whi[rows(b), rows(a)] = hi
        wlo[rows(b), rows(a)] = lo

    def relay(pick):
        for slot in range(8):
            k = cls[pick(GATHER[slot])]
            _, _, is_up, is_down = relayed(k, slot, low)

            @pl.when(is_up | is_down)
            def _():
                relay_copy(k, slot, is_up).start()

    def put_own(pick):
        def step(slot, _):
            k = class_at(GATHER, pick, slot)
            i, off = slot_row(k, slot)
            b = k + 8 * off - c + MID

            @pl.when((b >= 0) & (b < BW))
            def _():
                put(gat[k, slot], i - c + MID, b)
            return 0

        lax.fori_loop(0, 8, step, 0)

    def put_relayed(pick):
        def step(slot, _):
            k = class_at(GATHER, pick, slot)
            i, off, from_below, from_above = relayed(k, slot, 1 - low)

            @pl.when(from_below | from_above)
            def _():
                relay_copy(k, slot, from_below).wait_recv()
                shift = jnp.where(from_below, -8, 8) - c + MID
                put(rel[k, slot], i + shift, k + 8 * off + shift)
            return 0

        lax.fori_loop(0, 8, step, 0)

    w0 = lambda o: 0
    w1 = lambda o: o[0]
    w2 = lambda o: o[1]
    w3 = lambda o: o[2]
    w12 = lambda o: o[0] | o[1]
    w13 = lambda o: o[0] | o[2]
    w23 = lambda o: o[1] | o[2]
    w123 = lambda o: 7
    relay(w0)

    zero = jnp.zeros((bs, bs), BF16)
    for g in range(BW // GROUP):
        lo_b, hi_b = max(0, GROUP * g - MID), min(BW - 1, GROUP * g + GROUP - 1 + MID)
        for a in range(GROUP * g, GROUP * g + GROUP):
            for b in range(lo_b, hi_b + 1):
                if abs(a - b) > MID:
                    whi[a * bs:(a + 1) * bs, b * bs:(b + 1) * bs] = zero
                    wlo[a * bs:(a + 1) * bs, b * bs:(b + 1) * bs] = zero
    put_own(w0)

    def arrive(slot, delta):
        k = cls[delta]
        pltpu.make_async_remote_copy(
            src_ref=gat.at[k, slot], dst_ref=gat.at[k, slot],
            send_sem=gss.at[slot, 0], recv_sem=grs.at[slot, delta],
            device_id=(r, cls[1]), device_id_type=MESH,
        ).wait_recv()

    def wave(pick, dims):
        for slot in range(8):
            o = GATHER[slot]
            arrive(slot, pick(o))
            for n in dims:
                start_forward(slot, pick(o), o[n])

    wave(w1, (1,))
    for slot in range(8):
        start_forward(slot, 0, GATHER[slot][2])
        start_forward(slot, GATHER[slot][0], GATHER[slot][2])
    relay(w1)
    spread(w0)
    put_relayed(w0)
    put_own(w1)
    wave(w2, (2,))
    relay(w2)
    spread(w1)
    put_relayed(w1)
    wave(w12, (2,))
    relay(w12)
    spread(w2)
    put_own(w2)
    put_spread(w0)
    spread(w12)
    put_spread(w1)
    put_own(w12)
    put_relayed(w2)
    wave(w3, ())
    relay(w3)
    put_own(w3)
    put_relayed(w12)
    put_spread(w2)
    wave(w13, ())
    relay(w13)
    put_own(w13)
    put_spread(w12)
    put_relayed(w3)
    spread(w3)
    put_spread(w3)
    spread(w13)
    put_spread(w13)
    wave(w23, ())
    relay(w23)
    put_own(w23)
    put_relayed(w13)
    wave(w123, ())
    relay(w123)
    put_own(w123)
    spread(w23)
    put_spread(w23)
    put_relayed(w23)
    spread(w123)
    put_spread(w123)
    put_relayed(w123)

    def put_h(x, a):
        hi, lo = split(x * msk[pl.ds(a, 1), :])
        xhi[rows(a), bs:2 * bs] = hi
        xlo[rows(a), bs:2 * bs] = lo

    def h_copy(i):
        return pltpu.make_async_remote_copy(
            src_ref=h_ref.at[i, 0], dst_ref=hal.at[i],
            send_sem=hss.at[i], recv_sem=hrs.at[i],
            device_id=up, device_id_type=MESH,
        )

    def take_h(i, _):
        put_h(h_ref[i, own_slot(i)], i - c + MID)

        @pl.when(i != c)
        def _():
            h_copy(i).wait_recv()
            put_h(hal[i], i - c + jnp.where(i > c, -1, 15))
        return 0

    lax.fori_loop(0, 8, take_h, 0)

    xhi[:, 0:bs] = whi[:, MID * bs:(MID + 1) * bs]
    xlo[:, 0:bs] = wlo[:, MID * bs:(MID + 1) * bs]

    def product(g, vhi, vlo):
        lo_b, hi_b = max(0, GROUP * g - MID), min(BW - 1, GROUP * g + GROUP - 1 + MID)
        rs = slice(GROUP * g * bs, GROUP * (g + 1) * bs)
        ks = slice(lo_b * bs, (hi_b + 1) * bs)
        dot = functools.partial(jnp.dot, preferred_element_type=F32)
        return dot(whi[rs, ks], vhi[ks, :]) + dot(whi[rs, ks], vlo[ks, :]) + dot(wlo[rs, ks], vhi[ks, :])

    def mx_copy(a, back):
        return pltpu.make_async_remote_copy(
            src_ref=mx.at[a], dst_ref=rmx.at[back],
            send_sem=mss.at[a], recv_sem=mrs.at[back],
            device_id=owner(a), device_id_type=MESH,
        )

    for g in GROUPS:
        y = product(g, xhi, xlo)
        for n in range(GROUP):
            a = GROUP * g + n
            m = msk[a:a + 1, :]
            mx[a] = y[n * bs:(n + 1) * bs, bs:2 * bs] * m
            if a != MID:
                mx_copy(a, BW - 1 - a).start()
            x = y[n * bs:(n + 1) * bs, 0:bs] * m
            sq[a] = x
            hi, lo = split(x)
            x2s[a * bs:(a + 1) * bs, 0:bs] = hi
            x2s[a * bs:(a + 1) * bs, bs:2 * bs] = lo

    def half_product(g, v):
        lo_b, hi_b = max(0, GROUP * g - MID), min(BW - 1, GROUP * g + GROUP - 1 + MID)
        rs = slice(GROUP * g * bs, GROUP * (g + 1) * bs)
        ks = slice(lo_b * bs, (hi_b + 1) * bs)
        dot = functools.partial(jnp.dot, preferred_element_type=F32)
        y = dot(whi[rs, ks], v[ks, :])
        return y[:, 0:bs] + y[:, bs:2 * bs] + dot(wlo[rs, ks], v[ks, 0:bs])

    def out_copy(which, a):
        row, i = owner(a)
        return pltpu.make_async_remote_copy(
            src_ref=oc.at[which, a], dst_ref=ro.at[which, i],
            send_sem=oss.at[which, a], recv_sem=ors.at[which, i],
            device_id=(row, c), device_id_type=MESH,
        )

    def leaves(a):
        return (c + 1 + a < 8) | (c + 1 + a >= 16)

    def send_out(which, a):
        if a != MID:
            @pl.when(leaves(a))
            def _():
                out_copy(which, a).start()

    for g in GROUPS:
        y = half_product(g, x2s)
        for n in range(GROUP):
            a = GROUP * g + n
            oc[0, a] = 3.0 * sq[a] - 2.0 * (y[n * bs:(n + 1) * bs, :] * msk[a:a + 1, :])
            send_out(0, a)

    def put_mx(x, a):
        hi, lo = split(x.T)
        x2m[rows(a), 0:bs] = hi
        x2m[rows(a), bs:2 * bs] = lo

    put_mx(mx[MID], MID)
    for a in range(BW):
        if a != MID:
            mx_copy(BW - 1 - a, a).wait_recv()
            put_mx(rmx[a], a)

    for g in GROUPS:
        y = half_product(g, x2m)
        for n in range(GROUP):
            a = GROUP * g + n
            oc[1, a] = y[n * bs:(n + 1) * bs, :] * msk[a:a + 1, :]
            send_out(1, a)

    def finish(which, ref):
        def step(i, _):
            t = own_slot(i)
            ref[i, t] = oc[which, i - c + MID]

            @pl.when(i == c)
            def _():
                ref[i, 0] = jnp.zeros((bs, bs), F32)

            @pl.when(i != c)
            def _():
                pltpu.make_async_remote_copy(
                    src_ref=oc.at[which, 0], dst_ref=ro.at[which, i],
                    send_sem=oss.at[which, 0], recv_sem=ors.at[which, i],
                    device_id=up, device_id_type=MESH,
                ).wait_recv()
                ref[i, 1 - t] = ro[which, i]
            return 0

        lax.fori_loop(0, 8, step, 0)

    finish(0, new_ref)
    finish(1, en_ref)

    for cp in sends:
        cp.wait_send()

    def sent_h(i, _):
        @pl.when(i != c)
        def _():
            h_copy(i).wait_send()
        return 0

    lax.fori_loop(0, 8, sent_h, 0)

    def sent_relay(n, _):
        k = n // 8
        slot = n % 8
        _, _, is_up, is_down = relayed(k, slot, low)

        @pl.when(is_up | is_down)
        def _():
            relay_copy(k, slot, is_up).wait_send()
        return 0

    lax.fori_loop(0, 64, sent_relay, 0)
    for a in range(BW):
        if a != MID:
            mx_copy(a, BW - 1 - a).wait_send()

            @pl.when(leaves(a))
            def _():
                for which in (0, 1):
                    out_copy(which, a).wait_send()

    def cross_sent(slot, _):
        @pl.when(reach(c, slot, 1 - low) > 0)
        def _():
            cross_copy(slot).wait_send()
        return 0

    lax.fori_loop(0, 8, cross_sent, 0)
    for slot in range(8):
        for delta in range(8):
            spread_sent(slot, delta)


def body(density, hamiltonian, neighbours):
    bs = density.shape[-1]
    block = (bs, bs)
    wide = (BW * bs, BW * bs)
    tall = (BW * bs, 2 * bs)
    vm = pl.BlockSpec(memory_space=pltpu.VMEM)
    dma = pltpu.SemaphoreType.DMA
    out = jax.ShapeDtypeStruct(density.shape, F32)
    return pl.pallas_call(
        kernel,
        out_shape=(out, out),
        in_specs=[vm] * 3,
        out_specs=(vm, vm),
        scratch_shapes=[
            pltpu.VMEM((8, 8) + block, F32),
            pltpu.VMEM((8, 8) + block, F32),
            pltpu.VMEM((8, 8) + block, F32),
            pltpu.VMEM((8,) + block, F32),
            pltpu.VMEM(wide, BF16),
            pltpu.VMEM(wide, BF16),
            pltpu.VMEM(tall, BF16),
            pltpu.VMEM(tall, BF16),
            pltpu.VMEM(tall, BF16),
            pltpu.VMEM(tall, BF16),
            pltpu.VMEM((BW,) + block, F32),
            pltpu.VMEM((BW,) + block, F32),
            pltpu.VMEM((BW,) + block, F32),
            pltpu.VMEM((2, BW) + block, F32),
            pltpu.VMEM((2, 8) + block, F32),
            pltpu.VMEM((24, bs), F32),
            dma((8, 7)), dma((8, 8)),
            dma((8, 8)), dma((8, 8)),
            dma((8, 8, 3)), dma((8, 8)), dma((8,)),
            dma((8,)), dma((8,)),
            dma((BW,)), dma((BW,)),
            dma((2, BW)), dma((2, 8)),
        ],
        compiler_params=pltpu.CompilerParams(
            collective_id=0, has_side_effects=True, vmem_limit_bytes=44 * 2**20
        ),
        cost_estimate=pl.CostEstimate(flops=9 * 10**9, bytes_accessed=4 * 2**20, transcendentals=0),
        name="purify",
    )(density, hamiltonian, neighbours)


def solution(mesh):
    placed = (P("row", "col", None, None), P("row", "col", None, None), P("row", None))
    return jax.shard_map(
        body,
        mesh=mesh,
        in_specs=placed,
        out_specs=(P("row", "col", None, None), P("row", "col", None, None)),
        check_vma=False,
    )
```

time: 104 us -> 95.7 us (0.920)
  Pallas kernels: 100 us -> 89.8 us
  local copies, waits for them, and re-layouts: 3.36 us -> 5.07 us
    pallas_call x1, Pallas kernels: 100 us -> 89.8 us  [body(): pl.pallas_call(kernel, out_shape=(out, out), in_specs=[vm] * 3, out_specs...]
    unnamed x4 -> x8, local copies, waits for them, and re-layouts: 3.36 us -> 5.07 us
where the time goes in v2:
time: 95.7 us; the launch traced here: 95.5 us
  Pallas kernels  89.8 us (94%)
  local copies, waits for them, and re-layouts  5.07 us (5%)
    pallas_call x1, Pallas kernels, body(): pl.pallas_call(kernel, out_shape=(out, out), in_specs=[vm] * 3, out_specs...  89.8 us
    unnamed x8, local copies, waits for them, and re-layouts  5.07 us

profile of v2, /device:TPU:26, one launch (start us, length us, event | category | flops | bytes accessed | tf_op | source)
XLA Modules:
  0.0 95.5 jit_solution(14021172336822345818)
XLA Ops:
  0.6 0.0 copy-start
  0.6 1.2 %copy-done = f32[8,2,128,128]{3,2,1,0:T(8,128)S(1)} copy-done((f32[8,2,128,128]{3,2,1,0:T(8,128)S(1)}, f32[8,2,128,128]{3,2,1,0:T(8,128)}, u32[]{:S(2)}) %copy-start) | copy-done | bytes 1048600
  1.9 0.0 copy-start.1
  1.9 1.2 %copy-done.1 = f32[8,2,128,128]{3,2,1,0:T(8,128)S(1)} copy-done((f32[8,2,128,128]{3,2,1,0:T(8,128)S(1)}, f32[8,2,128,128]{3,2,1,0:T(8,128)}, u32[]{:S(2)}) %copy-start.1) | copy-done | bytes 1048600
  3.1 0.0 copy-start.2
  3.1 0.7 copy-done.2
  3.8 89.8 %purify.1 = (f32[8,2,128,128]{3,2,1,0:T(8,128)S(1)}, f32[8,2,128,128]{3,2,1,0:T(8,128)S(1)}) custom-call(f32[8,2,128,128]{3,2,1,0:T(8,128)S(1)} %copy-done, f32[8,2,128,128]{3,2,1,0:T(8,128)S(1)} %copy-done.1, s32[8,16]{1,0:T(8,128)S(1)} %copy-done.2), custom_call_target="tpu_custom_call" | custom-call | flops 8999999488 | bytes 4194304 | tf_op jit(solution)/shard_map/purify/pallas_call | solution.py:566
  93.5 1.0 %copy.7 = f32[8,2,128,128]{3,2,1,0:T(8,128)} copy(f32[8,2,128,128]{3,2,1,0:T(8,128)S(1)} %get-tuple-element.4) | data formatting | bytes 2097152
  94.5 1.0 %copy.8 = f32[8,2,128,128]{3,2,1,0:T(8,128)} copy(f32[8,2,128,128]{3,2,1,0:T(8,128)S(1)} %get-tuple-element.5) | data formatting | bytes 2097152
Async XLA Ops:
  0.6 1.2 %copy-start = (f32[8,2,128,128]{3,2,1,0:T(8,128)S(1)}, f32[8,2,128,128]{3,2,1,0:T(8,128)}, u32[]{:S(2)}) copy-start(f32[8,2,128,128]{3,2,1,0:T(8,128)} %d_ref.1) | copy-start | bytes 3145732
  1.9 1.2 %copy-start.1 = (f32[8,2,128,128]{3,2,1,0:T(8,128)S(1)}, f32[8,2,128,128]{3,2,1,0:T(8,128)}, u32[]{:S(2)}) copy-start(f32[8,2,128,128]{3,2,1,0:T(8,128)} %h_ref.1) | copy-start | bytes 3145732
  3.1 0.7 copy-start.2

commit v3 on v2

--- a/solution.py
+++ b/solution.py
@@ -16,8 +16,8 @@
 MID = 7
 GATHER = tuple(((1, 2, 4), (4, 1, 2), (2, 4, 1))[n % 3] for n in range(8))
 SPREAD = ((4, 2, 1), (2, 4, 1), (2, 4, 1), (4, 2, 1), (1, 2, 4), (4, 2, 1), (1, 2, 4), (1, 2, 4))
-GROUPS = (0, 4, 1, 3, 2)
-GROUP = 3
+PAIRS = (6, 8, 4, 10, 2, 12, 0, 14)
+LEAVE = (0, 14, 1, 13, 2, 12, 3, 11, 4, 10, 5, 9, 6, 8, 7)
 
 
 def class_of(c, delta):
@@ -72,11 +72,18 @@
 
 
 def kernel(
-    d_ref, h_ref, nb_ref, new_ref, en_ref,
-    gat, rel, ext, hal, whi, wlo, xhi, xlo, x2s, x2m, sq, mx, rmx, oc, ro, msk,
+    d_hbm, h_hbm, nb_hbm, new_ref, en_ref,
+    d_ref, h_ref, nb_ref, isem,
+    gat, rel, ext, hal, whi, wlo, xp, xh, x2s, x2m, sq, mx, rmx, oc, ro, msk,
     gss, grs, rss, rrs, ess, ers, zss, hss, hrs, mss, mrs, oss, ors,
 ):
     bs = d_ref.shape[-1]
+    fetch = [
+        pltpu.make_async_copy(src, dst, isem.at[n])
+        for n, (src, dst) in enumerate(((nb_hbm, nb_ref), (d_hbm, d_ref), (h_hbm, h_ref)))
+    ]
+    for cp in fetch:
+        cp.start()
     r = lax.axis_index("row")
     c = lax.axis_index("col")
     above = jnp.where(r == N_ROW - 1, 0, r + 1)
@@ -103,6 +110,7 @@
     def own_slot(i):
         return jnp.where(i <= c, 1, 0)
 
+    fetch[0].wait()
     col_mine = (8 * r + c - MID + NB + lax.broadcasted_iota(jnp.int32, (16, 16), 0)) % NB
     hit = jnp.where(nb_ref[pl.ds(c, 1), :] == col_mine, 1.0, 0.0).astype(F32)
     msk[0:16, :] = jnp.broadcast_to(jnp.max(hit, axis=1, keepdims=True), (16, bs))
@@ -119,6 +127,7 @@
         gat[c, slot] = d_ref[i, t] * m
         return 0
 
+    fetch[1].wait()
     lax.fori_loop(0, 8, contribute, 0)
     pl.semaphore_wait(barrier, 16)
 
@@ -184,8 +193,8 @@
 
     onward = {}
 
-    def spread(pick):
-        for slot in range(8):
+    def spread(pick, slots=range(8)):
+        for slot in slots:
             o = SPREAD[slot]
             delta = pick(o)
             k = cls[delta]
@@ -219,7 +228,7 @@
             k = jnp.where(hit, cls[delta], k)
         return k
 
-    def put_spread(pick):
+    def put_spread(pick, slots=range(8)):
         def step(slot, _):
             k = class_at(SPREAD, pick, slot)
 
@@ -229,7 +238,7 @@
                 put(ext[k, slot], i - c + MID + base, k + 8 * off - c + MID + base)
             return 0
 
-        lax.fori_loop(0, 8, step, 0)
+        lax.fori_loop(slots[0], slots[-1] + 1, step, 0)
 
     def send_h(i, _):
         @pl.when(i != c)
@@ -242,6 +251,7 @@
             ).start()
         return 0
 
+    fetch[2].wait()
     lax.fori_loop(0, 8, send_h, 0)
 
     def relayed(k, slot, inner_up):
@@ -260,9 +270,8 @@
         hi, lo = split(x)
         whi[rows(a), rows(b)] = hi
         wlo[rows(a), rows(b)] = lo
-        hi, lo = split(x.T)
-        whi[rows(b), rows(a)] = hi
-        wlo[rows(b), rows(a)] = lo
+        whi[rows(b), rows(a)] = hi.T
+        wlo[rows(b), rows(a)] = lo.T
 
     def relay(pick):
         for slot in range(8):
@@ -286,10 +295,14 @@
 
         lax.fori_loop(0, 8, step, 0)
 
-    def put_relayed(pick):
+    def put_relayed(pick, inner=True, outer=True):
         def step(slot, _):
             k = class_at(GATHER, pick, slot)
             i, off, from_below, from_above = relayed(k, slot, 1 - low)
+            if not outer:
+                from_below, from_above = from_below & (low == 0), from_above & (low == 1)
+            if not inner:
+                from_below, from_above = from_below & (low == 1), from_above & (low == 0)
 
             @pl.when(from_below | from_above)
             def _():
@@ -311,13 +324,13 @@
     relay(w0)
 
     zero = jnp.zeros((bs, bs), BF16)
-    for g in range(BW // GROUP):
-        lo_b, hi_b = max(0, GROUP * g - MID), min(BW - 1, GROUP * g + GROUP - 1 + MID)
-        for a in range(GROUP * g, GROUP * g + GROUP):
-            for b in range(lo_b, hi_b + 1):
-                if abs(a - b) > MID:
-                    whi[a * bs:(a + 1) * bs, b * bs:(b + 1) * bs] = zero
-                    wlo[a * bs:(a + 1) * bs, b * bs:(b + 1) * bs] = zero
+    for b in range(0, BW, 2):
+        b1 = min(b + 1, BW - 1)
+        for a in range(max(0, b - MID), min(BW - 1, b1 + MID) + 1):
+            for q in (b, b1):
+                if abs(a - q) > MID:
+                    whi[a * bs:(a + 1) * bs, q * bs:(q + 1) * bs] = zero
+                    wlo[a * bs:(a + 1) * bs, q * bs:(q + 1) * bs] = zero
     put_own(w0)
 
     def arrive(slot, delta):
@@ -356,38 +369,47 @@
     put_spread(w1)
     put_own(w12)
     put_relayed(w2)
+    diag = range(0, 4)
+    rest = range(4, 8)
     wave(w3, ())
     relay(w3)
     put_own(w3)
-    put_relayed(w12)
+    put_relayed(w12, outer=False)
     put_spread(w2)
     wave(w13, ())
     relay(w13)
     put_own(w13)
     put_spread(w12)
-    put_relayed(w3)
-    spread(w3)
-    put_spread(w3)
-    spread(w13)
-    put_spread(w13)
+    put_relayed(w3, outer=False)
+    for w in (w3, w13):
+        spread(w, rest)
+        put_spread(w, rest)
     wave(w23, ())
     relay(w23)
     put_own(w23)
-    put_relayed(w13)
+    put_relayed(w13, outer=False)
     wave(w123, ())
     relay(w123)
     put_own(w123)
-    spread(w23)
-    put_spread(w23)
-    put_relayed(w23)
-    spread(w123)
-    put_spread(w123)
-    put_relayed(w123)
+    put_relayed(w23, outer=False)
+    for w in (w23, w123):
+        spread(w, rest)
+        put_spread(w, rest)
+    put_relayed(w123, outer=False)
+
+    def outer_diagonal():
+        for w in (w12, w3, w13):
+            put_relayed(w, inner=False)
+        for w in (w3, w13, w23, w123):
+            spread(w, diag)
+            put_spread(w, diag)
+        for w in (w23, w123):
+            put_relayed(w, inner=False)
 
     def put_h(x, a):
         hi, lo = split(x * msk[pl.ds(a, 1), :])
-        xhi[rows(a), bs:2 * bs] = hi
-        xlo[rows(a), bs:2 * bs] = lo
+        xh[rows(a), 0:bs] = hi
+        xh[rows(a), bs:2 * bs] = lo
 
     def h_copy(i):
         return pltpu.make_async_remote_copy(
@@ -407,15 +429,12 @@
 
     lax.fori_loop(0, 8, take_h, 0)
 
-    xhi[:, 0:bs] = whi[:, MID * bs:(MID + 1) * bs]
-    xlo[:, 0:bs] = wlo[:, MID * bs:(MID + 1) * bs]
-
-    def product(g, vhi, vlo):
-        lo_b, hi_b = max(0, GROUP * g - MID), min(BW - 1, GROUP * g + GROUP - 1 + MID)
-        rs = slice(GROUP * g * bs, GROUP * (g + 1) * bs)
-        ks = slice(lo_b * bs, (hi_b + 1) * bs)
-        dot = functools.partial(jnp.dot, preferred_element_type=F32)
-        return dot(whi[rs, ks], vhi[ks, :]) + dot(whi[rs, ks], vlo[ks, :]) + dot(wlo[rs, ks], vhi[ks, :])
+
+    dot = functools.partial(jnp.dot, preferred_element_type=F32)
+
+    def band(a):
+        lo_b, hi_b = max(0, a - MID), min(BW - 1, a + MID)
+        return slice(a * bs, (a + 1) * bs), slice(lo_b * bs, (hi_b + 1) * bs)
 
     def mx_copy(a, back):
         return pltpu.make_async_remote_copy(
@@ -424,27 +443,43 @@
             device_id=owner(a), device_id_type=MESH,
         )
 
-    for g in GROUPS:
-        y = product(g, xhi, xlo)
-        for n in range(GROUP):
-            a = GROUP * g + n
-            m = msk[a:a + 1, :]
-            mx[a] = y[n * bs:(n + 1) * bs, bs:2 * bs] * m
+    def half(a, v):
+        rs, ks = band(a)
+        y = dot(whi[rs, ks], v[ks, :])
+        return y[:, 0:bs] + y[:, bs:2 * bs] + dot(wlo[rs, ks], v[ks, 0:bs])
+
+    def first_product(some):
+        for a in some:
+            mx[a] = half(a, xh) * msk[a:a + 1, :]
             if a != MID:
                 mx_copy(a, BW - 1 - a).start()
-            x = y[n * bs:(n + 1) * bs, 0:bs] * m
-            sq[a] = x
-            hi, lo = split(x)
-            x2s[a * bs:(a + 1) * bs, 0:bs] = hi
-            x2s[a * bs:(a + 1) * bs, bs:2 * bs] = lo
-
-    def half_product(g, v):
-        lo_b, hi_b = max(0, GROUP * g - MID), min(BW - 1, GROUP * g + GROUP - 1 + MID)
-        rs = slice(GROUP * g * bs, GROUP * (g + 1) * bs)
-        ks = slice(lo_b * bs, (hi_b + 1) * bs)
-        dot = functools.partial(jnp.dot, preferred_element_type=F32)
-        y = dot(whi[rs, ks], v[ks, :])
-        return y[:, 0:bs] + y[:, bs:2 * bs] + dot(wlo[rs, ks], v[ks, 0:bs])
+
+    @pl.when(low == 1)
+    def _():
+        first_product(range(BW - 1, MID - 1, -1))
+
+    @pl.when(low == 0)
+    def _():
+        first_product(range(0, MID + 1))
+
+    outer_diagonal()
+
+    @pl.when(low == 1)
+    def _():
+        first_product(range(MID - 1, -1, -1))
+
+    @pl.when(low == 0)
+    def _():
+        first_product(range(MID + 1, BW))
+
+    xp[:, 0:bs] = whi[:, MID * bs:(MID + 1) * bs]
+    xp[:, bs:2 * bs] = wlo[:, MID * bs:(MID + 1) * bs]
+    for a in LEAVE:
+        x = half(a, xp) * msk[a:a + 1, :]
+        sq[a] = x
+        hi, lo = split(x)
+        x2s[a * bs:(a + 1) * bs, 0:bs] = hi
+        x2s[a * bs:(a + 1) * bs, bs:2 * bs] = lo
 
     def out_copy(which, a):
         row, i = owner(a)
@@ -463,30 +498,36 @@
             def _():
                 out_copy(which, a).start()
 
-    for g in GROUPS:
-        y = half_product(g, x2s)
-        for n in range(GROUP):
-            a = GROUP * g + n
-            oc[0, a] = 3.0 * sq[a] - 2.0 * (y[n * bs:(n + 1) * bs, :] * msk[a:a + 1, :])
-            send_out(0, a)
+    for a in LEAVE:
+        y = half(a, x2s)
+        oc[0, a] = 3.0 * sq[a] - 2.0 * (y * msk[a:a + 1, :])
+        send_out(0, a)
 
     def put_mx(x, a):
-        hi, lo = split(x.T)
-        x2m[rows(a), 0:bs] = hi
-        x2m[rows(a), bs:2 * bs] = lo
+        hi, lo = split(x)
+        x2m[rows(a), 0:bs] = hi.T
+        x2m[rows(a), bs:2 * bs] = lo.T
 
     put_mx(mx[MID], MID)
-    for a in range(BW):
-        if a != MID:
-            mx_copy(BW - 1 - a, a).wait_recv()
-            put_mx(rmx[a], a)
-
-    for g in GROUPS:
-        y = half_product(g, x2m)
-        for n in range(GROUP):
-            a = GROUP * g + n
-            oc[1, a] = y[n * bs:(n + 1) * bs, :] * msk[a:a + 1, :]
-            send_out(1, a)
+    touched = set()
+    for b in PAIRS:
+        b1 = min(b + 1, BW - 1)
+        for a in range(b, b1 + 1):
+            if a != MID:
+                mx_copy(BW - 1 - a, a).wait_recv()
+                put_mx(rmx[a], a)
+        ks = slice(b * bs, (b1 + 1) * bs)
+        lo_a, hi_a = max(0, b - MID), min(BW - 1, b1 + MID)
+        rs = slice(lo_a * bs, (hi_a + 1) * bs)
+        y = dot(whi[rs, ks], x2m[ks, :])
+        y = y[:, 0:bs] + y[:, bs:2 * bs] + dot(wlo[rs, ks], x2m[ks, 0:bs])
+        for a in range(lo_a, hi_a + 1):
+            v = y[(a - lo_a) * bs:(a - lo_a + 1) * bs, :]
+            oc[1, a] = oc[1, a] + v if a in touched else v
+            touched.add(a)
+    for a in LEAVE:
+        oc[1, a] = oc[1, a] * msk[a:a + 1, :]
+        send_out(1, a)
 
     def finish(which, ref):
         def step(i, _):
@@ -566,9 +607,13 @@
     return pl.pallas_call(
         kernel,
         out_shape=(out, out),
-        in_specs=[vm] * 3,
+        in_specs=[pl.BlockSpec(memory_space=pltpu.HBM)] * 3,
         out_specs=(vm, vm),
         scratch_shapes=[
+            pltpu.VMEM(density.shape, F32),
+            pltpu.VMEM(hamiltonian.shape, F32),
+            pltpu.VMEM(neighbours.shape, jnp.int32),
+            dma((3,)),
             pltpu.VMEM((8, 8) + block, F32),
             pltpu.VMEM((8, 8) + block, F32),
             pltpu.VMEM((8, 8) + block, F32),
@@ -593,7 +638,7 @@
             dma((2, BW)), dma((2, 8)),
         ],
         compiler_params=pltpu.CompilerParams(
-            collective_id=0, has_side_effects=True, vmem_limit_bytes=44 * 2**20
+            collective_id=0, has_side_effects=True, vmem_limit_bytes=52 * 2**20
         ),
         cost_estimate=pl.CostEstimate(flops=9 * 10**9, bytes_accessed=4 * 2**20, transcendentals=0),
         name="purify",

time: 95.7 us -> 92.6 us (0.968)
  Pallas kernels: 89.8 us -> 87.6 us
  local copies, waits for them, and re-layouts: 5.07 us -> 3.25 us
    pallas_call x1, Pallas kernels: 89.8 us -> 87.6 us  [body(): pl.pallas_call(kernel, out_shape=(out, out), in_specs=[pl.BlockSpec(memor...]
    unnamed x8 -> x6, local copies, waits for them, and re-layouts: 5.07 us -> 3.25 us
where the time goes in v3:
time: 92.6 us; the launch traced here: 91.5 us
  Pallas kernels  87.6 us (95%)
  local copies, waits for them, and re-layouts  3.25 us (4%)
    pallas_call x1, Pallas kernels, body(): pl.pallas_call(kernel, out_shape=(out, out), in_specs=[pl.BlockSpec(memor...  87.6 us
    unnamed x6, local copies, waits for them, and re-layouts  3.25 us

profile of v3, /device:TPU:26, one launch (start us, length us, event | category | flops | bytes accessed | tf_op | source)
XLA Modules:
  0.0 91.5 jit_solution(11358796369107076693)
XLA Ops:
  0.6 0.0 copy-start
  0.6 0.7 copy-done
  1.3 87.6 %purify.1 = (f32[8,2,128,128]{3,2,1,0:T(8,128)S(1)}, f32[8,2,128,128]{3,2,1,0:T(8,128)}) custom-call(f32[8,2,128,128]{3,2,1,0:T(8,128)} %d_hbm.1, f32[8,2,128,128]{3,2,1,0:T(8,128)} %h_hbm.1, s32[8,16]{1,0:T(8,128)S(1)} %copy-done), custom_call_target="tpu_custom_call" | custom-call | flops 8999999488 | bytes 4194304 | tf_op jit(solution)/shard_map/purify/pallas_call | solution.py:607
  88.9 0.0 copy-start.1
  88.9 1.0 %copy.7 = f32[8,2,128,128]{3,2,1,0:T(8,128)} copy(f32[8,2,128,128]{3,2,1,0:T(8,128)S(1)} %get-tuple-element.4) | data formatting | bytes 2097152
  89.9 0.6 copy-done.1
  90.5 1.0 %copy.8 = f32[8,2,128,128]{3,2,1,0:T(8,128)} copy(f32[8,2,128,128]{3,2,1,0:T(8,128)S(1)} %copy-done.1) | data formatting | bytes 2097152
Async XLA Ops:
  0.6 0.7 copy-start
  88.9 1.6 %copy-start.1 = (f32[8,2,128,128]{3,2,1,0:T(8,128)S(1)}, f32[8,2,128,128]{3,2,1,0:T(8,128)}, u32[]{:S(2)}) copy-start(f32[8,2,128,128]{3,2,1,0:T(8,128)} %get-tuple-element.5) | copy-start | bytes 3145732

commit v4 on v3

--- a/solution.py
+++ b/solution.py
@@ -362,18 +362,18 @@
     put_relayed(w1)
     wave(w12, (2,))
     relay(w12)
+    wave(w3, ())
+    relay(w3)
     spread(w2)
     put_own(w2)
     put_spread(w0)
     spread(w12)
     put_spread(w1)
     put_own(w12)
+    put_own(w3)
     put_relayed(w2)
     diag = range(0, 4)
     rest = range(4, 8)
-    wave(w3, ())
-    relay(w3)
-    put_own(w3)
     put_relayed(w12, outer=False)
     put_spread(w2)
     wave(w13, ())
@@ -381,9 +381,6 @@
     put_own(w13)
     put_spread(w12)
     put_relayed(w3, outer=False)
-    for w in (w3, w13):
-        spread(w, rest)
-        put_spread(w, rest)
     wave(w23, ())
     relay(w23)
     put_own(w23)
@@ -392,7 +389,7 @@
     relay(w123)
     put_own(w123)
     put_relayed(w23, outer=False)
-    for w in (w23, w123):
+    for w in (w3, w13, w23, w123):
         spread(w, rest)
         put_spread(w, rest)
     put_relayed(w123, outer=False)

time: 92.6 us -> 92.7 us (level)
  no operation moved by 1% of the time
where the time goes in v4:
time: 92.7 us; the launch traced here: 91.3 us
  Pallas kernels  87.4 us (94%)
  local copies, waits for them, and re-layouts  3.25 us (4%)
    pallas_call x1, Pallas kernels, body(): pl.pallas_call(kernel, out_shape=(out, out), in_specs=[pl.BlockSpec(memor...  87.4 us
    unnamed x6, local copies, waits for them, and re-layouts  3.25 us

profile of v4, /device:TPU:26, one launch (start us, length us, event | category | flops | bytes accessed | tf_op | source)
XLA Modules:
  0.0 91.3 jit_solution(664985661023724206)
XLA Ops:
  0.6 0.0 copy-start
  0.6 0.7 copy-done
  1.3 87.4 %purify.1 = (f32[8,2,128,128]{3,2,1,0:T(8,128)S(1)}, f32[8,2,128,128]{3,2,1,0:T(8,128)}) custom-call(f32[8,2,128,128]{3,2,1,0:T(8,128)} %d_hbm.1, f32[8,2,128,128]{3,2,1,0:T(8,128)} %h_hbm.1, s32[8,16]{1,0:T(8,128)S(1)} %copy-done), custom_call_target="tpu_custom_call" | custom-call | flops 8999999488 | bytes 4194304 | tf_op jit(solution)/shard_map/purify/pallas_call | solution.py:604
  88.8 0.0 copy-start.1
  88.8 1.0 %copy.7 = f32[8,2,128,128]{3,2,1,0:T(8,128)} copy(f32[8,2,128,128]{3,2,1,0:T(8,128)S(1)} %get-tuple-element.4) | data formatting | bytes 2097152
  89.7 0.6 copy-done.1
  90.4 1.0 %copy.8 = f32[8,2,128,128]{3,2,1,0:T(8,128)} copy(f32[8,2,128,128]{3,2,1,0:T(8,128)S(1)} %copy-done.1) | data formatting | bytes 2097152
Async XLA Ops:
  0.6 0.7 copy-start
  88.8 1.6 %copy-start.1 = (f32[8,2,128,128]{3,2,1,0:T(8,128)S(1)}, f32[8,2,128,128]{3,2,1,0:T(8,128)}, u32[]{:S(2)}) copy-start(f32[8,2,128,128]{3,2,1,0:T(8,128)} %get-tuple-element.5) | copy-start | bytes 3145732
